TPU v7x, 512 devices: a whole 4x8x8 slice. The times are simulated.
512 devices in a mesh: dp: 16 (over y, x_hi), expert: 32 (over z, x_lo, core).
Axes of the slice: x: 4 (x_hi: 2, x_lo: 2; x = x_hi * 2 + x_lo), y: 8, z: 8, core: 2. Of those that a mesh axis runs over, the one named last changes fastest.
Arguments:
- acts: bfloat16 [32, 2048, 2560], P('expert', 'dp'), may hold values from -6 to 6
- out_grads: bfloat16 [32, 2048, 768], P('expert', 'dp'), may hold values from -1 to 1
- next_tokens: bfloat16 [32, 2048, 2560], P('expert', 'dp'), may hold values from -6 to 6
- master: float32 [32, 2560, 768], P('expert', 'dp'), may hold values from -0.125 to 0.125
- first_moment: float32 [32, 2560, 768], P('expert', 'dp'), may hold values from -6 to 6
- second_moment: float32 [32, 2560, 768], P('expert', 'dp'), may hold values from 0.5 to 20
- counts: int32 [16, 160], P('dp'), may hold values from 32 to 128
- selected: int32 [32], replicated, may hold values from 0 to 159
- old_place: int32 [32], replicated, may hold values from 0 to 31, each once
- new_place: int32 [32], replicated, may hold values from 0 to 31, each once
Outputs:
- new_master: float32 [32, 2560, 768], P('expert', 'dp')
- new_first: float32 [32, 2560, 768], P('expert', 'dp')
- new_second: float32 [32, 2560, 768], P('expert', 'dp')
- forward: bfloat16 [32, 2048, 768], P('expert', 'dp')
Inputs may be any that keep to these rules, and one draw needn't show every extreme that they name: `old_place`: each holder index appears once. `new_place`: each holder index appears once.
All inputs are finite; a program needn't handle non-finite values.
Results may differ from a plain program's by a relative error of at most 0.012.
Values may be sent and summed in bfloat16 or wider, within the bound.
A program may use at most 64 MiB of HBM per device.

v0:
```python
import jax
import jax.numpy as jnp
from jax import lax
from jax.sharding import Mesh
from jax.sharding import PartitionSpec as P

DP = ("dp_0", "dp_1")


beta_first = 0.9
beta_second = 0.95
bias_first = 1.0 - 0.9**10
bias_second = 1.0 - 0.95**10
learn_rate = 0.01
decay_rate = 0.1
epsilon = 1e-08


def in_one_piece(arrays, axis, split_dim, concat_dim, along):
    ends, at = ([], 0)
    for a in arrays[:-1]:
        at += a.shape[along]
        ends.append(at)
    both = jnp.concatenate(arrays, axis=along)
    return tuple(
        jnp.split(
            lax.all_to_all(both, axis, split_axis=split_dim, concat_axis=concat_dim, tiled=True),
            ends,
            axis=along,
        )
    )


def summed_rows(terms, axes):
    running = terms.astype(jnp.bfloat16)
    for axis in axes:
        running = lax.psum_scatter(running, axis, scatter_dimension=0, tiled=True)
    return running.astype(jnp.float32)


def whole_of(value, axes, dim):
    for axis in reversed(axes):
        value = lax.all_gather(value, axis, axis=dim, tiled=True)
    return value


def adamw(weights, moment_one, moment_two, gradient):
    moment_one = beta_first * moment_one + (1.0 - beta_first) * gradient
    moment_two = beta_second * moment_two + (1.0 - beta_second) * gradient * gradient
    update = (
        moment_one / bias_first / (jnp.sqrt(moment_two / bias_second) + epsilon)
        + decay_rate * weights
    )
    return (weights - learn_rate * update, moment_one, moment_two)


def relocate_states(weights, moment_one, moment_two, order):
    holders = lax.axis_size("expert")
    shard_rows, width = weights.shape
    first = weights.reshape(holders, shard_rows // holders, width)
    second = moment_one.reshape(holders, shard_rows // holders, width)
    third = moment_two.reshape(holders, shard_rows // holders, width)
    relayed = tuple(
        (
            part.astype(jnp.float32)
            for part in in_one_piece(
                (
                    first.astype(jnp.bfloat16),
                    second.astype(jnp.bfloat16),
                    third.astype(jnp.bfloat16),
                ),
                "expert",
                0,
                0,
                1,
            )
        )
    )
    arranged = tuple((jnp.take(member, order, axis=0) for member in relayed))
    arrived = tuple(
        (
            part.astype(jnp.float32)
            for part in in_one_piece(
                (
                    arranged[0].astype(jnp.bfloat16),
                    arranged[1].astype(jnp.bfloat16),
                    arranged[2].astype(jnp.bfloat16),
                ),
                "expert",
                0,
                0,
                1,
            )
        )
    )
    return tuple((member.reshape(shard_rows, width) for member in arrived))


def body(
    acts,
    out_grads,
    next_tokens,
    master,
    first_moment,
    second_moment,
    counts,
    selected,
    old_place,
    new_place,
):
    holders = lax.axis_size("expert")
    my_holder = lax.axis_index("expert")
    tokens_here = acts[0]
    grads_here = out_grads[0]
    positions = jnp.arange(holders, dtype=jnp.int32)
    expert_id = jnp.sum(jnp.where(old_place == my_holder, selected, 0))
    table = jnp.arange(counts.shape[1], dtype=jnp.int32)
    routed = jnp.sum(jnp.where(table == expert_id, counts[0], 0))
    live = jnp.arange(tokens_here.shape[0], dtype=jnp.int32) < routed
    masked = jnp.where(live[:, None], grads_here, jnp.zeros_like(grads_here))
    destination = jnp.sum(
        jnp.where(old_place[None, :] == positions[:, None], new_place[None, :], 0), axis=1
    )
    order = jnp.sum(
        jnp.where(destination[None, :] == positions[:, None], positions[None, :], 0), axis=1
    )
    columns = tokens_here
    gradient = summed_rows(
        lax.dot_general(
            columns, masked, (((0,), (0,)), ((), ())), preferred_element_type=jnp.float32
        ),
        DP,
    )
    updated = adamw(master[0], first_moment[0], second_moment[0], gradient)
    weights, moment_one, moment_two = relocate_states(updated[0], updated[1], updated[2], order)
    lowered = weights.astype(jnp.bfloat16)
    incoming = next_tokens[0]
    columns = incoming
    forward = jnp.dot(columns, whole_of(lowered, DP, 0), preferred_element_type=jnp.float32)
    return (weights[None], moment_one[None], moment_two[None], forward.astype(jnp.bfloat16)[None])


def solution(mesh):
    finer = Mesh(mesh.devices.reshape(8, 2, mesh.shape["expert"]), ("dp_0", "dp_1", "expert"))
    in_specs = (
        P("expert", DP, None),
        P("expert", DP, None),
        P("expert", DP, None),
        P("expert", DP, None),
        P("expert", DP, None),
        P("expert", DP, None),
        P(DP, None),
        P(),
        P(),
        P(),
    )
    out_specs = (
        P("expert", DP, None),
        P("expert", DP, None),
        P("expert", DP, None),
        P("expert", DP, None),
    )
    return jax.shard_map(body, mesh=finer, in_specs=in_specs, out_specs=out_specs, check_vma=False)
```

profile of v0, /device:TPU:1, one launch (start us, length us, event | category | flops | bytes accessed | tf_op | source)
XLA Modules:
  0.0 244.2 jit_solution(14914969079745127046)
XLA Ops:
  7.2 0.0 copy-start
  7.2 0.0 reduce-scatter.7.cloned.1.call-start
  7.2 1.4 fusion.16
  8.6 2.0 fusion.15
  10.6 0.6 iota_compare_fusion.2
  11.2 0.0 copy-done
  11.2 4.1 %fusion = bf16[2560,768]{0,1:T(8,128)(2,1)} fusion(bf16[1,128,2560]{2,1,0:T(8,128)(2,1)S(1)} %copy-done, bf16[1,128,768]{2,1,0:T(8,128)(2,1)} %param.13, pred[128]{0:T(512)(128)(4,1)S(1)} %iota_compare_fusion.2), kind=kOutput, calls=%fused_computation.4 | convolution fusion | flops 505380864 | bytes 4784256 | tf_op jit(solution)/shard_map/dot_general | solution.py:129
  15.3 6.3 %copy.44 = bf16[2560,768]{1,0:T(8,128)(2,1)} copy(bf16[2560,768]{0,1:T(8,128)(2,1)} %fusion) | data formatting | bytes 7864320
  21.6 0.0 reduce-scatter.7.cloned.1.call-update
  21.6 0.0 reduce-scatter.9.cloned.1.call-start
  21.7 60.8 %reduce-scatter.7.cloned.1.call-done = bf16[320,768]{1,0:T(8,128)(2,1)} async-done(((bf16[2560,768]{1,0:T(8,128)(2,1)}), bf16[320,768]{1,0:T(8,128)(2,1)}) %reduce-scatter.7.cloned.1.call-update) | async-done | bytes 491536
  82.5 0.0 reduce-scatter.9.cloned.1.call-update
  82.5 25.5 %reduce-scatter.9.cloned.1.call-done = bf16[160,768]{1,0:T(8,128)(2,1)} async-done(((bf16[320,768]{1,0:T(8,128)(2,1)}), bf16[160,768]{1,0:T(8,128)(2,1)}) %reduce-scatter.9.cloned.1.call-update) | async-done | bytes 245776 | tf_op jit(solution)/shard_map/reduce_scatter | solution.py:37
  108.0 0.0 copy-done.1
  108.0 0.0 copy-done.2
  108.0 0.0 copy-done.3
  108.0 1.4 fusion.8
  109.4 0.1 convert_element_type.62
  109.5 0.1 convert_element_type.64
  109.6 0.1 convert_element_type.66
  109.7 0.0 copy-start.4
  109.7 0.0 copy-start.6
  109.7 1.3 pad_maximum_fusion
  111.1 8.2 %all-to-all-start = ((bf16[32,15,768]{2,1,0:T(8,128)(2,1)}), bf16[32,15,768]{2,1,0:T(8,128)(2,1)S(1)}, u32[]{:S(2)}, u32[]{:S(2)}) async-start(bf16[32,15,768]{2,1,0:T(8,128)(2,1)} %pad_maximum_fusion), calls=%async_computation | async-start | bytes 1572864 | tf_op jit(solution)/shard_map/all_to_all | solution.py:27
  119.3 0.0 all-gather.2.cloned.1.call-start
  119.3 0.0 copy-done.4
  119.3 0.0 copy-done.6
  119.3 0.1 select_reduce_fusion.1
  119.4 0.1 select_reduce_fusion
  119.6 22.3 %all-to-all-done = bf16[32,15,768]{2,1,0:T(8,128)(2,1)S(1)} async-done(((bf16[32,15,768]{2,1,0:T(8,128)(2,1)}), bf16[32,15,768]{2,1,0:T(8,128)(2,1)S(1)}, u32[]{:S(2)}, u32[]{:S(2)}) %all-to-all-start) | async-done | bytes 737312 | tf_op jit(solution)/shard_map/all_to_all | solution.py:27
  141.9 0.2 fusion.19
  142.1 0.6 gather_fusion
  142.7 0.6 gather_fusion.1
  143.2 0.6 gather_fusion.2
  143.8 0.3 select_convert_fusion.2
  144.1 0.4 pad_maximum_fusion.1
  144.5 26.6 %all_to_all.10 = bf16[32,15,768]{2,1,0:T(8,128)(2,1)S(1)} all-to-all(bf16[32,15,768]{2,1,0:T(8,128)(2,1)S(1)} %pad_maximum_fusion.1), channel_id=1, replica_groups=mesh['dp_0'=8,'dp_1'=2,'expert'=32] {'expert'}, dimensions={0} | all-to-all | bytes 1474560 | tf_op jit(solution)/shard_map/all_to_all | solution.py:27
  171.1 0.2 fusion.18
  171.3 0.8 convert_element_type.73
  172.1 9.5 %all_gather.6 = bf16[320,768]{1,0:T(8,128)(2,1)} all-gather(bf16[160,768]{1,0:T(8,128)(2,1)} %convert_element_type.73), channel_id=1, replica_groups=mesh['dp_0'=8,'dp_1'=2,'expert'=32] {'dp_1'}, dimensions={0}, use_global_device_ids=true | all-gather | bytes 737280 | tf_op jit(solution)/shard_map/all_gather | solution.py:43
  181.6 0.0 all-gather.2.cloned.1.call-update
  181.7 0.9 reshape.40
  182.5 0.9 reshape.41
  183.4 0.9 reshape.42
  184.3 49.2 %all-gather.2.cloned.1.call-done = bf16[2560,768]{1,0:T(8,128)(2,1)} async-done(((bf16[320,768]{1,0:T(8,128)(2,1)}), bf16[2560,768]{1,0:T(8,128)(2,1)}) %all-gather.2.cloned.1.call-update) | async-done | bytes 3932176 | tf_op jit(solution)/shard_map/all_gather | solution.py:43
  233.5 0.0 copy-done.5
  233.5 3.3 %fusion.1 = bf16[1,128,768]{1,2,0:T(8,128)(2,1)S(1)} fusion(bf16[2560,768]{1,0:T(8,128)(2,1)} %all-gather.2.cloned.1.call-done, bf16[1,128,2560]{2,1,0:T(8,128)(2,1)S(1)} %copy-done.5), kind=kOutput, calls=%fused_computation.6 | convolution fusion | flops 503414784 | bytes 4784128 | tf_op jit(solution)/shard_map/dot_general | solution.py:139
  236.8 0.8 copy.43
  (7 shorter events, 0.0 us)
Async XLA Ops:
  7.2 4.0 %copy-start = (bf16[1,128,2560]{2,1,0:T(8,128)(2,1)S(1)}, bf16[1,128,2560]{2,1,0:T(8,128)(2,1)}, u32[]{:S(2)}) copy-start(bf16[1,128,2560]{2,1,0:T(8,128)(2,1)} %param.12) | copy-start | bytes 1966084
  7.2 75.3 %reduce-scatter.7.cloned.1.call-start = ((), (), s32[]{:S(2)}) async-start(), calls=%async_computation.5 | async-start | bytes 4423680
  21.6 86.4 %copy-start.1 = (f32[1,160,768]{2,1,0:T(8,128)S(1)}, f32[1,160,768]{2,1,0:T(8,128)}, u32[]{:S(2)}) copy-start(f32[1,160,768]{2,1,0:T(8,128)} %param.15) | copy-start | bytes 1474564
  21.6 86.4 %copy-start.2 = (f32[1,160,768]{2,1,0:T(8,128)S(1)}, f32[1,160,768]{2,1,0:T(8,128)}, u32[]{:S(2)}) copy-start(f32[1,160,768]{2,1,0:T(8,128)} %param.16) | copy-start | bytes 1474564
  21.6 86.4 %copy-start.3 = (f32[1,160,768]{2,1,0:T(8,128)S(1)}, f32[1,160,768]{2,1,0:T(8,128)}, u32[]{:S(2)}) copy-start(f32[1,160,768]{2,1,0:T(8,128)} %param.17) | copy-start | bytes 1474564
  21.6 86.4 %reduce-scatter.9.cloned.1.call-start = ((), (), s32[]{:S(2)}) async-start(), calls=%async_computation.6 | async-start | bytes 737280 | tf_op jit(solution)/shard_map/reduce_scatter | solution.py:37
  109.7 9.6 %copy-start.4 = (s32[32]{0:T(128)S(1)}, s32[32]{0:T(128)}, u32[]{:S(2)}) copy-start(s32[32]{0:T(128)} %param.20) | copy-start | bytes 388
  109.7 9.6 %copy-start.6 = (s32[32]{0:T(128)S(1)}, s32[32]{0:T(128)}, u32[]{:S(2)}) copy-start(s32[32]{0:T(128)} %param.21) | copy-start | bytes 388
  111.1 30.8 %all-to-all-start = ((bf16[32,15,768]{2,1,0:T(8,128)(2,1)}), bf16[32,15,768]{2,1,0:T(8,128)(2,1)S(1)}, u32[]{:S(2)}, u32[]{:S(2)}) async-start(bf16[32,15,768]{2,1,0:T(8,128)(2,1)} %pad_maximum_fusion), calls=%async_computation | async-start | bytes 1572864 | tf_op jit(solution)/shard_map/all_to_all | solution.py:27
  119.3 114.2 %all-gather.2.cloned.1.call-start = ((), (), s32[]{:S(2)}) async-start(), calls=%async_computation.4 | async-start | bytes 4423680 | tf_op jit(solution)/shard_map/all_gather | solution.py:43
  182.5 51.0 %copy-start.5 = (bf16[1,128,2560]{2,1,0:T(8,128)(2,1)S(1)}, bf16[1,128,2560]{2,1,0:T(8,128)(2,1)}, u32[]{:S(2)}) copy-start(bf16[1,128,2560]{2,1,0:T(8,128)(2,1)} %param.14) | copy-start | bytes 1966084
Sparse Core Ops, SparseCore 0:
  21.7 60.6 reduce-scatter.6
  85.3 22.6 reduce-scatter.8
  181.8 51.6 all-gather.1
where the time goes:
time: 245 us; the launch traced here: 244 us
  waiting for transfers between devices  158 us (64%)
  blocking collectives  36.1 us (15%)
  between operations  13.9 us (6%)
  local copies, waits for them, and re-layouts  12.8 us (5%)
  starting transfers between devices  8.32 us (3%)
  other arithmetic  7.79 us (3%)
  matrix products  7.44 us (3%)
    unnamed x4, waiting for transfers between devices  60.8 us
    all_gather x1, waiting for transfers between devices, whole_of(): value = lax.all_gather(value, axis, axis=dim, tiled=True)  49.2 us
    all_to_all x1, blocking collectives, in_one_piece(): lax.all_to_all(both, axis, split_axis=split_dim, concat_axis=concat_dim,...  26.6 us
    reduce_scatter x1, waiting for transfers between devices, summed_rows(): running = lax.psum_scatter(running, axis, scatter_dimension=0, tiled=True)  25.5 us
    all_to_all x1, waiting for transfers between devices, in_one_piece(): lax.all_to_all(both, axis, split_axis=split_dim, concat_axis=concat_dim,...  22.3 us
    all_gather x1, blocking collectives, whole_of(): value = lax.all_gather(value, axis, axis=dim, tiled=True)  9.53 us
    all_to_all x1, starting transfers between devices, in_one_piece(): lax.all_to_all(both, axis, split_axis=split_dim, concat_axis=concat_dim,...  8.2 us
    unnamed x16, local copies, waits for them, and re-layouts  7.13 us
  transfers between devices with their start and end apart: 4, of which 4 were waited for; matrix products, arithmetic and copies ran while one was open for 1% of the time, Pallas kernels for 0%

commit v1 on v0

v1 whole, which is shorter than its diff:
```python
import jax
import jax.numpy as jnp
from jax import lax
from jax.experimental import pallas as pl
from jax.experimental.pallas import tpu as pltpu
from jax.sharding import PartitionSpec as P

MESH = pl.DeviceIdType.MESH

beta_first = 0.9
beta_second = 0.95
bias_first = 1.0 - 0.9**10
bias_second = 1.0 - 0.95**10
learn_rate = 0.01
decay_rate = 0.1
epsilon = 1e-08

RING = 8
ROWS = 160
WIDE = 384
TOK = 128
HOLD = 32
RELAYS = 30
F32 = jnp.float32
BF16 = jnp.bfloat16
CHAINS = ((0, 1, 4), (1, -1, 4), (1, 1, 3), (0, -1, 3))


def adamw(weights, moment_one, moment_two, gradient):
    moment_one = beta_first * moment_one + (1.0 - beta_first) * gradient
    moment_two = beta_second * moment_two + (1.0 - beta_second) * gradient * gradient
    update = (
        moment_one / bias_first / (jnp.sqrt(moment_two / bias_second) + epsilon)
        + decay_rate * weights
    )
    return (weights - learn_rate * update, moment_one, moment_two)


def kernel(
    counts, selected, old_place, new_place,
    acts, grads, tokens, master, first, second,
    out_w, out_m, out_v, out_f,
    order, at, nt, at_in, nt_in, ntx, g_own, g_in, term,
    rs_out, rs_in, stage_w, relay_a, relay_b, sorted_w, stage_m, relay_m, sorted_m, new_w, new_m,
    gathered, f_out, f_in, f_own,
    x_send, x_recv, rs_send, rs_recv, ag_send, ag_recv, p_send, p_recv, f_send, f_recv,
):
    dp, me = lax.axis_index("dp"), lax.axis_index("expert")
    relay_w = (relay_a, relay_b)
    y, par = dp // 2, dp % 2
    other = 1 - par
    partner = (y * 2 + other, me)
    up = (((y + 1) % RING) * 2 + par, me)
    down = (((y + RING - 1) % RING) * 2 + par, me)

    barrier = pltpu.get_barrier_semaphore()
    for peer in (partner, up, down):
        pl.semaphore_signal(barrier, inc=1, device_id=peer, device_id_type=MESH)

    def greet(j, c):
        pl.semaphore_signal(
            barrier, inc=1, device_id=(dp, (me + j) % HOLD), device_id_type=MESH
        )
        return c

    lax.fori_loop(1, HOLD, greet, 0)

    def push(src, dst, send, recv, to):
        copy = pltpu.make_async_remote_copy(
            src_ref=src, dst_ref=dst, send_sem=send, recv_sem=recv,
            device_id=to, device_id_type=MESH,
        )
        copy.start()

    def got(ref, sem):
        pltpu.make_async_copy(ref, ref, sem).wait()

    def all_but(ref, sems, count, mine):
        def go(n, c):
            @pl.when(n != mine)
            def _():
                got(ref.at[n], sems.at[n])

            return c

        lax.fori_loop(0, count, go, 0)

    def find(i, c):
        return c + jnp.where(old_place[i] == me, selected[i], 0)

    expert_id = lax.fori_loop(0, HOLD, find, jnp.int32(0))
    routed = counts[0, expert_id]
    live = lax.broadcasted_iota(jnp.int32, (TOK, 768), 0) < routed
    value = grads[...]
    g_own[...] = jnp.where(live, value, jnp.zeros_like(value))

    def turned(src, dst):
        for i in range(20):
            tile = src[:, i * 128 : (i + 1) * 128].T
            for m in range(4):
                row = i * 128 + m * 32
                block, at_row = row // ROWS, row % ROWS
                dst[block % 2, block // 2, at_row : at_row + 32, :] = tile[m * 32 : (m + 1) * 32]

    turned(acts, at)
    pl.semaphore_wait(barrier, 3 + HOLD - 1)

    push(g_own, g_in, x_send.at[8], x_recv.at[8], partner)
    for k in (4, 3, 5, 2, 6, 1, 7, 0):
        t = (y + k) % RING
        push(at.at[other, t], at_in.at[k], x_send.at[k], x_recv.at[k], partner)
    turned(tokens, nt)
    push(nt.at[other], nt_in, x_send.at[9], x_recv.at[9], partner)

    def place(d, c):
        def look(i, c):
            return c + jnp.where(new_place[i] == d, old_place[i], 0)

        order[d] = lax.fori_loop(0, HOLD, look, jnp.int32(0), unroll=True)
        return c

    lax.fori_loop(0, HOLD, place, 0)

    def contribution(k, h):
        t = (y + k) % RING
        cols = slice(h * WIDE, (h + 1) * WIDE)
        return jnp.dot(at[par, t], g_own[:, cols], preferred_element_type=F32) + jnp.dot(
            at_in[k], g_in[:, cols], preferred_element_type=F32
        )

    got(g_in, x_recv.at[8])
    arrived = set()
    for s in range(4):
        for c, (h, way, hops) in enumerate(CHAINS):
            if s >= hops:
                continue
            k = (way * (hops - s)) % RING
            if k not in arrived:
                arrived.add(k)
                got(at_in.at[k], x_recv.at[k])
            own = contribution(k, h)
            if s == 0:
                rs_out[c, s] = own.astype(BF16)
            else:
                term[...] = own
                got(rs_in.at[c, s - 1], rs_recv.at[c, s - 1])
                rs_out[c, s] = (rs_in[c, s - 1].astype(F32) + term[...]).astype(BF16)
            push(
                rs_out.at[c, s], rs_in.at[c, s], rs_send.at[c, s], rs_recv.at[c, s],
                up if way == 1 else down,
            )
    got(at_in.at[0], x_recv.at[0])

    def one_phase_out(stage, relay, send, recv, first_relay):
        def go(n, c):
            j = n + first_relay

            @pl.when(j != me)
            def _():
                push(stage.at[n], relay.at[me], send.at[n], recv.at[me], (dp, j))

            return c

        lax.fori_loop(0, RELAYS, go, 0)

    for h in range(2):
        term[...] = contribution(0, h)
        for c, (half, way, hops) in enumerate(CHAINS):
            if half == h:
                got(rs_in.at[c, hops - 1], rs_recv.at[c, hops - 1])
        ends = [(c, hops - 1) for c, (half, _, hops) in enumerate(CHAINS) if half == h]
        for k in range(10):
            for q in range(3):
                rows = slice(16 * k, 16 * k + 16)
                local = slice(128 * q, 128 * q + 128)
                cols = slice(h * WIDE + 128 * q, h * WIDE + 128 * q + 128)
                total = term[rows, local]
                for c, s in ends:
                    total = total + rs_in[c, s, rows, local].astype(F32)
                w, m, v = adamw(master[rows, cols], first[rows, cols], second[rows, cols], total)
                p = 3 * k + q
                stage_w[h, p] = w.astype(BF16)
                stage_m[p, 2 * h] = m.astype(BF16)
                stage_m[p, 2 * h + 1] = v.astype(BF16)
        one_phase_out(stage_w.at[h], relay_w[h], p_send.at[0, h], p_recv.at[0, h], 0)

        @pl.when(me < RELAYS)
        def _():
            relay_w[h][me] = stage_w[h, me]

    one_phase_out(stage_m, relay_m, p_send.at[0, 2], p_recv.at[0, 2], 2)

    @pl.when(me >= 2)
    def _():
        relay_m[me] = stage_m[me - 2]

    def two_phase_out(relay, ordered, final, send, recv, first_relay):
        slot = me - first_relay

        @pl.when((me >= first_relay) & (me < first_relay + RELAYS))
        def _():
            all_but(relay, recv[0], HOLD, me)

            def go(d, c):
                ordered[d] = relay[order[d]]

                @pl.when(d != me)
                def _():
                    push(ordered.at[d], final.at[slot], send[1].at[d], recv[1].at[slot], (dp, d))

                return c

            lax.fori_loop(0, HOLD, go, 0)
            final[slot] = ordered[me]

    def two_phase_in(final, recv, first_relay):
        all_but(final, recv, RELAYS, me - first_relay)

    for h in range(2):
        two_phase_out(
            relay_w[h], sorted_w.at[h], new_w.at[h],
            (p_send.at[0, h], p_send.at[1, h]), (p_recv.at[0, h], p_recv.at[1, h]), 0,
        )
    for h in range(2):
        two_phase_in(new_w.at[h], p_recv.at[1, h], 0)
        for p in range(RELAYS):
            k, q = p // 3, p % 3
            gathered[h, y, 16 * k : 16 * k + 16, 128 * q : 128 * q + 128] = new_w[h, p]
        for c, (half, way, hops) in enumerate(CHAINS):
            if half == h:
                mine = gathered.at[h, y]
                push(mine, mine, ag_send.at[c, 0], ag_recv.at[c, 0], up if way == 1 else down)
    two_phase_out(
        relay_m, sorted_m, new_m,
        (p_send.at[0, 2], p_send.at[1, 2]), (p_recv.at[0, 2], p_recv.at[1, 2]), 2,
    )
    for p in range(RELAYS):
        k, q = p // 3, p % 3
        for h in range(2):
            cols = slice(h * WIDE + 128 * q, h * WIDE + 128 * q + 128)
            out_w[16 * k : 16 * k + 16, cols] = new_w[h, p].astype(F32)

    got(nt_in, x_recv.at[9])
    for i in range(10):
        ntx[0:128, 128 * i : 128 * i + 128] = jnp.concatenate(
            [nt_in[(128 * i + 32 * m) // ROWS, (128 * i + 32 * m) % ROWS : (128 * i + 32 * m) % ROWS + 32] for m in range(4)], axis=0
        ).T
        ntx[128:256, 128 * i : 128 * i + 128] = jnp.concatenate(
            [nt[par, (128 * i + 32 * m) // ROWS, (128 * i + 32 * m) % ROWS : (128 * i + 32 * m) % ROWS + 32] for m in range(4)], axis=0
        ).T

    for s in range(1, 5):
        for c, (h, way, hops) in enumerate(CHAINS):
            if s > hops:
                continue
            block = gathered.at[h, (y - way * s) % RING]
            got(block, ag_recv.at[c, s - 1])
            if s < hops:
                push(block, block, ag_send.at[c, s], ag_recv.at[c, s], up if way == 1 else down)

    for h in range(2):
        whole = gathered[h].reshape(RING * ROWS, WIDE)
        f_out[h] = jnp.dot(ntx[0:128], whole, preferred_element_type=F32).astype(BF16)
        push(f_out.at[h], f_in.at[h], f_send.at[h], f_recv.at[h], partner)
    for h in range(2):
        whole = gathered[h].reshape(RING * ROWS, WIDE)
        f_own[h] = jnp.dot(ntx[128:256], whole, preferred_element_type=F32)

    two_phase_in(new_m, p_recv.at[1, 2], 2)
    for p in range(RELAYS):
        k, q = p // 3, p % 3
        for h in range(2):
            cols = slice(h * WIDE + 128 * q, h * WIDE + 128 * q + 128)
            out_m[16 * k : 16 * k + 16, cols] = new_m[p, 2 * h].astype(F32)
            out_v[16 * k : 16 * k + 16, cols] = new_m[p, 2 * h + 1].astype(F32)

    for h in range(2):
        got(f_in.at[h], f_recv.at[h])
        out_f[:, h * WIDE : (h + 1) * WIDE] = (f_own[h] + f_in[h].astype(F32)).astype(BF16)

    for k in range(8):
        got(at_in.at[0], x_send.at[k])
    got(g_own, x_send.at[8])
    got(nt_in, x_send.at[9])
    for c, (h, way, hops) in enumerate(CHAINS):
        for s in range(hops):
            got(rs_out.at[c, s], rs_send.at[c, s])
            got(gathered.at[0, 0], ag_send.at[c, s])
    for h in range(2):
        got(f_out.at[h], f_send.at[h])

    def sent(stage, relay, one, two, first_relay):
        all_but(stage, one, RELAYS, me - first_relay)

        @pl.when((me >= first_relay) & (me < first_relay + RELAYS))
        def _():
            all_but(relay, two, HOLD, me)

    for h in range(2):
        sent(stage_w.at[h], relay_w[h], p_send.at[0, h], p_send.at[1, h], 0)
    sent(stage_m, relay_m, p_send.at[0, 2], p_send.at[1, 2], 2)


def body(
    acts, out_grads, next_tokens, master, first_moment, second_moment,
    counts, selected, old_place, new_place,
):
    vmem = pl.BlockSpec(memory_space=pltpu.VMEM)
    smem = pl.BlockSpec(memory_space=pltpu.SMEM)
    state = jax.ShapeDtypeStruct((ROWS, 768), F32)
    w, m, v, f = pl.pallas_call(
        kernel,
        out_shape=(state, state, state, jax.ShapeDtypeStruct((TOK, 768), BF16)),
        in_specs=[smem] * 4 + [vmem] * 6,
        out_specs=(vmem,) * 4,
        scratch_shapes=[
            pltpu.SMEM((HOLD,), jnp.int32),
            pltpu.VMEM((2, RING, ROWS, TOK), BF16),
            pltpu.VMEM((2, RING, ROWS, TOK), BF16),
            pltpu.VMEM((RING, ROWS, TOK), BF16),
            pltpu.VMEM((RING, ROWS, TOK), BF16),
            pltpu.VMEM((2 * TOK, RING * ROWS), BF16),
            pltpu.VMEM((TOK, 768), BF16),
            pltpu.VMEM((TOK, 768), BF16),
            pltpu.VMEM((ROWS, WIDE), F32),
            pltpu.VMEM((4, 4, ROWS, WIDE), BF16),
            pltpu.VMEM((4, 4, ROWS, WIDE), BF16),
            pltpu.VMEM((2, RELAYS, 16, 128), BF16),
            pltpu.VMEM((HOLD, 16, 128), BF16),
            pltpu.VMEM((HOLD, 16, 128), BF16),
            pltpu.VMEM((2, HOLD, 16, 128), BF16),
            pltpu.VMEM((RELAYS, 4, 16, 128), BF16),
            pltpu.VMEM((HOLD, 4, 16, 128), BF16),
            pltpu.VMEM((HOLD, 4, 16, 128), BF16),
            pltpu.VMEM((2, RELAYS, 16, 128), BF16),
            pltpu.VMEM((RELAYS, 4, 16, 128), BF16),
            pltpu.VMEM((2, RING, ROWS, WIDE), BF16),
            pltpu.VMEM((2, TOK, WIDE), BF16),
            pltpu.VMEM((2, TOK, WIDE), BF16),
            pltpu.VMEM((2, TOK, WIDE), F32),
            pltpu.SemaphoreType.DMA((10,)),
            pltpu.SemaphoreType.DMA((10,)),
            pltpu.SemaphoreType.DMA((4, 4)),
            pltpu.SemaphoreType.DMA((4, 4)),
            pltpu.SemaphoreType.DMA((4, 4)),
            pltpu.SemaphoreType.DMA((4, 4)),
            pltpu.SemaphoreType.DMA((2, 3, HOLD)),
            pltpu.SemaphoreType.DMA((2, 3, HOLD)),
            pltpu.SemaphoreType.DMA((2,)),
            pltpu.SemaphoreType.DMA((2,)),
        ],
        compiler_params=pltpu.CompilerParams(
            collective_id=0, has_side_effects=True, vmem_limit_bytes=48 * 2**20
        ),
    )(
        counts, selected, old_place, new_place,
        acts[0], out_grads[0], next_tokens[0], master[0], first_moment[0], second_moment[0],
    )
    return w[None], m[None], v[None], f[None]


def solution(mesh):
    both = P("expert", "dp", None)
    return jax.shard_map(
        body,
        mesh=mesh,
        in_specs=(both,) * 6 + (P("dp", None), P(), P(), P()),
        out_specs=(both,) * 4,
        check_vma=False,
    )
```

time: 245 us -> 109 us (0.44)
  waiting for transfers between devices: 158 us -> 0 us
  Pallas kernels: 0 us -> 96.5 us
  blocking collectives: 36.1 us -> 0 us
  between operations: 13.9 us -> 0.68 us
  starting transfers between devices: 8.32 us -> 0 us
  other arithmetic: 7.79 us -> 0 us
  matrix products: 7.44 us -> 0 us
  local copies, waits for them, and re-layouts: 12.8 us -> 9.88 us
    pallas_call x0 -> x1, Pallas kernels: none -> 96.5 us  [body(): pl.pallas_call(kernel, out_shape=(state, state, state, jax.ShapeDtypeStru...]
    unnamed x4 -> x0, waiting for transfers between devices: 60.8 us -> none
    all_gather x1 -> x0, waiting for transfers between devices: 49.2 us -> none  [whole_of(): value = lax.all_gather(value, axis, axis=dim, tiled=True)]
    all_to_all x1 -> x0, blocking collectives: 26.6 us -> none  [in_one_piece(): lax.all_to_all(both, axis, split_axis=split_dim, concat_axis=concat_dim,...]
    reduce_scatter x1 -> x0, waiting for transfers between devices: 25.5 us -> none  [summed_rows(): running = lax.psum_scatter(running, axis, scatter_dimension=0, tiled=True)]
    all_to_all x1 -> x0, waiting for transfers between devices: 22.3 us -> none  [in_one_piece(): lax.all_to_all(both, axis, split_axis=split_dim, concat_axis=concat_dim,...]
    all_gather x1 -> x0, blocking collectives: 9.53 us -> none  [whole_of(): value = lax.all_gather(value, axis, axis=dim, tiled=True)]
    all_to_all x1 -> x0, starting transfers between devices: 8.2 us -> none  [in_one_piece(): lax.all_to_all(both, axis, split_axis=split_dim, concat_axis=concat_dim,...]
  transfers between devices with their start and end apart: 4 -> 0, of which waited for: 4 -> 0; matrix products, arithmetic and copies ran while one was open for 1% -> 0% of each run, Pallas kernels for 0% -> 0%
where the time goes in v1:
time: 109 us; the launch traced here: 107 us
  Pallas kernels  96.5 us (89%)
  local copies, waits for them, and re-layouts  9.88 us (9%)
    pallas_call x1, Pallas kernels, body(): pl.pallas_call(kernel, out_shape=(state, state, state, jax.ShapeDtypeStru...  96.5 us
    unnamed x24, local copies, waits for them, and re-layouts  9.88 us

profile of v1, /device:TPU:1, one launch (start us, length us, event | category | flops | bytes accessed | tf_op | source)
XLA Modules:
  0.0 107.1 jit_solution(12468154623686233054)
XLA Ops:
  0.6 0.0 copy-start.8
  0.6 0.0 copy-start.9
  0.7 0.0 copy-start.6
  0.7 0.0 copy-start.7
  0.7 0.6 copy-done.8
  1.3 0.0 copy-done.9
  1.3 0.0 copy-done.6
  1.3 0.0 copy-done.7
  1.3 0.0 copy-start
  1.4 1.1 %copy-done = bf16[1,128,2560]{2,1,0:T(8,128)(2,1)S(1)} copy-done((bf16[1,128,2560]{2,1,0:T(8,128)(2,1)S(1)}, bf16[1,128,2560]{2,1,0:T(8,128)(2,1)}, u32[]{:S(2)}) %copy-start) | copy-done | bytes 655384
  2.4 0.0 copy-start.1
  2.4 1.1 %copy-done.1 = bf16[1,128,2560]{2,1,0:T(8,128)(2,1)S(1)} copy-done((bf16[1,128,2560]{2,1,0:T(8,128)(2,1)S(1)}, bf16[1,128,2560]{2,1,0:T(8,128)(2,1)}, u32[]{:S(2)}) %copy-start.1) | copy-done | bytes 655384
  3.5 0.0 copy-start.2
  3.5 1.0 copy-done.2
  4.6 0.0 copy-start.3
  4.6 1.0 copy-done.3
  5.6 0.0 copy-start.4
  5.6 1.0 copy-done.4
  6.6 0.0 copy-start.5
  6.6 0.9 copy-done.5
  7.5 96.5 %shard_map.129 = (f32[160,768]{1,0:T(8,128)S(1)}, f32[160,768]{1,0:T(8,128)S(1)}, f32[160,768]{1,0:T(8,128)S(1)}, bf16[128,768]{1,0:T(8,128)(2,1)S(1)}) custom-call(s32[1,160]{1,0:T(1,128)S(1)} %copy-done.6, s32[32]{0:T(128)S(1)} %copy-done.7, s32[32]{0:T(128)S(1)} %copy-done.8, s32[32]{0:T(128)S(1)} %copy-done.9, bf16[128,2560]{1,0:T(8,128)(2,1)S(1)} %bitcast.10, ...), custom_call_target="tpu_custom_call" | custom-call | tf_op jit(solution)/shard_map/pallas_call | solution.py:311
  104.1 0.8 copy.18
  104.8 0.8 copy.19
  105.6 0.8 copy.20
  106.4 0.7 copy.21
Async XLA Ops:
  0.6 0.7 copy-start.8
  0.6 0.7 copy-start.9
  0.7 0.7 copy-start.6
  0.7 0.7 copy-start.7
  1.3 1.1 %copy-start = (bf16[1,128,2560]{2,1,0:T(8,128)(2,1)S(1)}, bf16[1,128,2560]{2,1,0:T(8,128)(2,1)}, u32[]{:S(2)}) copy-start(bf16[1,128,2560]{2,1,0:T(8,128)(2,1)} %param.10) | copy-start | bytes 1966084
  2.4 1.1 %copy-start.1 = (bf16[1,128,2560]{2,1,0:T(8,128)(2,1)S(1)}, bf16[1,128,2560]{2,1,0:T(8,128)(2,1)}, u32[]{:S(2)}) copy-start(bf16[1,128,2560]{2,1,0:T(8,128)(2,1)} %param.12) | copy-start | bytes 1966084
  3.5 1.0 copy-start.2
  4.6 1.0 copy-start.3
  5.6 1.0 copy-start.4
  6.6 0.9 copy-start.5

commit v2 on v1

--- a/solution.py
+++ b/solution.py
@@ -37,9 +37,10 @@
 
 
 def kernel(
-    counts, selected, old_place, new_place,
-    acts, grads, tokens, master, first, second,
+    counts_hbm, selected_hbm, old_hbm, new_hbm,
+    acts_hbm, grads_hbm, tokens_hbm, master_hbm, first_hbm, second_hbm,
     out_w, out_m, out_v, out_f,
+    counts, selected, old_place, new_place, acts, grads, tokens, master, first, second, in_sem,
     order, at, nt, at_in, nt_in, ntx, g_own, g_in, term,
     rs_out, rs_in, stage_w, relay_a, relay_b, sorted_w, stage_m, relay_m, sorted_m, new_w, new_m,
     gathered, f_out, f_in, f_own,
@@ -53,6 +54,17 @@
     up = (((y + 1) % RING) * 2 + par, me)
     down = (((y + RING - 1) % RING) * 2 + par, me)
 
+    reads = [
+        pltpu.make_async_copy(src, dst, in_sem.at[i])
+        for i, (src, dst) in enumerate((
+            (counts_hbm, counts), (selected_hbm, selected), (old_hbm, old_place),
+            (new_hbm, new_place), (acts_hbm, acts), (grads_hbm, grads), (tokens_hbm, tokens),
+            (master_hbm, master), (first_hbm, first), (second_hbm, second),
+        ))
+    ]
+    for read in reads:
+        read.start()
+
     barrier = pltpu.get_barrier_semaphore()
     for peer in (partner, up, down):
         pl.semaphore_signal(barrier, inc=1, device_id=peer, device_id_type=MESH)
@@ -75,15 +87,8 @@
     def got(ref, sem):
         pltpu.make_async_copy(ref, ref, sem).wait()
 
-    def all_but(ref, sems, count, mine):
-        def go(n, c):
-            @pl.when(n != mine)
-            def _():
-                got(ref.at[n], sems.at[n])
-
-            return c
-
-        lax.fori_loop(0, count, go, 0)
+    for i in (0, 1, 2, 3, 5):
+        reads[i].wait()
 
     def find(i, c):
         return c + jnp.where(old_place[i] == me, selected[i], 0)
@@ -102,6 +107,7 @@
                 block, at_row = row // ROWS, row % ROWS
                 dst[block % 2, block // 2, at_row : at_row + 32, :] = tile[m * 32 : (m + 1) * 32]
 
+    reads[4].wait()
     turned(acts, at)
     pl.semaphore_wait(barrier, 3 + HOLD - 1)
 
@@ -109,6 +115,7 @@
     for k in (4, 3, 5, 2, 6, 1, 7, 0):
         t = (y + k) % RING
         push(at.at[other, t], at_in.at[k], x_send.at[k], x_recv.at[k], partner)
+    reads[6].wait()
     turned(tokens, nt)
     push(nt.at[other], nt_in, x_send.at[9], x_recv.at[9], partner)
 
@@ -157,12 +164,14 @@
 
             @pl.when(j != me)
             def _():
-                push(stage.at[n], relay.at[me], send.at[n], recv.at[me], (dp, j))
+                push(stage.at[n], relay.at[me], send, recv, (dp, j))
 
             return c
 
         lax.fori_loop(0, RELAYS, go, 0)
 
+    for i in (7, 8, 9):
+        reads[i].wait()
     for h in range(2):
         term[...] = contribution(0, h)
         for c, (half, way, hops) in enumerate(CHAINS):
@@ -188,25 +197,19 @@
         def _():
             relay_w[h][me] = stage_w[h, me]
 
-    one_phase_out(stage_m, relay_m, p_send.at[0, 2], p_recv.at[0, 2], 2)
-
-    @pl.when(me >= 2)
-    def _():
-        relay_m[me] = stage_m[me - 2]
-
     def two_phase_out(relay, ordered, final, send, recv, first_relay):
         slot = me - first_relay
 
         @pl.when((me >= first_relay) & (me < first_relay + RELAYS))
         def _():
-            all_but(relay, recv[0], HOLD, me)
+            got(relay.at[pl.ds(0, HOLD - 1)], recv[0])
 
             def go(d, c):
                 ordered[d] = relay[order[d]]
 
                 @pl.when(d != me)
                 def _():
-                    push(ordered.at[d], final.at[slot], send[1].at[d], recv[1].at[slot], (dp, d))
+                    push(ordered.at[d], final.at[slot], send[1], recv[1], (dp, d))
 
                 return c
 
@@ -214,7 +217,15 @@
             final[slot] = ordered[me]
 
     def two_phase_in(final, recv, first_relay):
-        all_but(final, recv, RELAYS, me - first_relay)
+        relaying = (me >= first_relay) & (me < first_relay + RELAYS)
+
+        @pl.when(relaying)
+        def _():
+            got(final.at[pl.ds(0, RELAYS - 1)], recv)
+
+        @pl.when(jnp.logical_not(relaying))
+        def _():
+            got(final, recv)
 
     for h in range(2):
         two_phase_out(
@@ -230,10 +241,12 @@
             if half == h:
                 mine = gathered.at[h, y]
                 push(mine, mine, ag_send.at[c, 0], ag_recv.at[c, 0], up if way == 1 else down)
-    two_phase_out(
-        relay_m, sorted_m, new_m,
-        (p_send.at[0, 2], p_send.at[1, 2]), (p_recv.at[0, 2], p_recv.at[1, 2]), 2,
-    )
+    one_phase_out(stage_m, relay_m, p_send.at[0, 2], p_recv.at[0, 2], 2)
+
+    @pl.when(me >= 2)
+    def _():
+        relay_m[me] = stage_m[me - 2]
+
     for p in range(RELAYS):
         k, q = p // 3, p % 3
         for h in range(2):
@@ -249,6 +262,11 @@
             [nt[par, (128 * i + 32 * m) // ROWS, (128 * i + 32 * m) % ROWS : (128 * i + 32 * m) % ROWS + 32] for m in range(4)], axis=0
         ).T
 
+    def forward_out(h):
+        whole = gathered[h].reshape(RING * ROWS, WIDE)
+        f_out[h] = jnp.dot(ntx[0:128], whole, preferred_element_type=F32).astype(BF16)
+        push(f_out.at[h], f_in.at[h], f_send.at[h], f_recv.at[h], partner)
+
     for s in range(1, 5):
         for c, (h, way, hops) in enumerate(CHAINS):
             if s > hops:
@@ -257,11 +275,13 @@
             got(block, ag_recv.at[c, s - 1])
             if s < hops:
                 push(block, block, ag_send.at[c, s], ag_recv.at[c, s], up if way == 1 else down)
-
-    for h in range(2):
-        whole = gathered[h].reshape(RING * ROWS, WIDE)
-        f_out[h] = jnp.dot(ntx[0:128], whole, preferred_element_type=F32).astype(BF16)
-        push(f_out.at[h], f_in.at[h], f_send.at[h], f_recv.at[h], partner)
+            if s == 4:
+                forward_out(h)
+        if s == 2:
+            two_phase_out(
+                relay_m, sorted_m, new_m,
+                (p_send.at[0, 2], p_send.at[1, 2]), (p_recv.at[0, 2], p_recv.at[1, 2]), 2,
+            )
     for h in range(2):
         whole = gathered[h].reshape(RING * ROWS, WIDE)
         f_own[h] = jnp.dot(ntx[128:256], whole, preferred_element_type=F32)
@@ -290,15 +310,39 @@
         got(f_out.at[h], f_send.at[h])
 
     def sent(stage, relay, one, two, first_relay):
-        all_but(stage, one, RELAYS, me - first_relay)
-
-        @pl.when((me >= first_relay) & (me < first_relay + RELAYS))
-        def _():
-            all_but(relay, two, HOLD, me)
+        relaying = (me >= first_relay) & (me < first_relay + RELAYS)
+
+        @pl.when(relaying)
+        def _():
+            got(stage.at[pl.ds(0, RELAYS - 1)], one)
+            got(relay.at[pl.ds(0, HOLD - 1)], two)
+
+        @pl.when(jnp.logical_not(relaying))
+        def _():
+            got(stage, one)
 
     for h in range(2):
         sent(stage_w.at[h], relay_w[h], p_send.at[0, h], p_send.at[1, h], 0)
     sent(stage_m, relay_m, p_send.at[0, 2], p_send.at[1, 2], 2)
+
+
+def write(w, m, v, f, out_w, out_m, out_v, out_f, w_held, m_held, v_held, f_held, sems):
+    held = (w_held, m_held, v_held, f_held)
+    reads = [
+        pltpu.make_async_copy(src, dst, sems.at[0, i])
+        for i, (src, dst) in enumerate(zip((w, m, v, f), held))
+    ]
+    writes = [
+        pltpu.make_async_copy(src, dst, sems.at[1, i])
+        for i, (src, dst) in enumerate(zip(held, (out_w, out_m, out_v, out_f)))
+    ]
+    for copy in reads:
+        copy.start()
+    for copy, after in zip(reads, writes):
+        copy.wait()
+        after.start()
+    for copy in writes:
+        copy.wait()
 
 
 def body(
@@ -306,14 +350,25 @@
     counts, selected, old_place, new_place,
 ):
     vmem = pl.BlockSpec(memory_space=pltpu.VMEM)
-    smem = pl.BlockSpec(memory_space=pltpu.SMEM)
+    anywhere = pl.BlockSpec(memory_space=pl.ANY)
     state = jax.ShapeDtypeStruct((ROWS, 768), F32)
     w, m, v, f = pl.pallas_call(
         kernel,
         out_shape=(state, state, state, jax.ShapeDtypeStruct((TOK, 768), BF16)),
-        in_specs=[smem] * 4 + [vmem] * 6,
+        in_specs=[anywhere] * 10,
         out_specs=(vmem,) * 4,
         scratch_shapes=[
+            pltpu.SMEM(counts.shape, jnp.int32),
+            pltpu.SMEM((HOLD,), jnp.int32),
+            pltpu.SMEM((HOLD,), jnp.int32),
+            pltpu.SMEM((HOLD,), jnp.int32),
+            pltpu.VMEM((TOK, 2560), BF16),
+            pltpu.VMEM((TOK, 768), BF16),
+            pltpu.VMEM((TOK, 2560), BF16),
+            pltpu.VMEM((ROWS, 768), F32),
+            pltpu.VMEM((ROWS, 768), F32),
+            pltpu.VMEM((ROWS, 768), F32),
+            pltpu.SemaphoreType.DMA((10,)),
             pltpu.SMEM((HOLD,), jnp.int32),
             pltpu.VMEM((2, RING, ROWS, TOK), BF16),
             pltpu.VMEM((2, RING, ROWS, TOK), BF16),
@@ -344,18 +399,27 @@
             pltpu.SemaphoreType.DMA((4, 4)),
             pltpu.SemaphoreType.DMA((4, 4)),
             pltpu.SemaphoreType.DMA((4, 4)),
-            pltpu.SemaphoreType.DMA((2, 3, HOLD)),
-            pltpu.SemaphoreType.DMA((2, 3, HOLD)),
+            pltpu.SemaphoreType.DMA((2, 3)),
+            pltpu.SemaphoreType.DMA((2, 3)),
             pltpu.SemaphoreType.DMA((2,)),
             pltpu.SemaphoreType.DMA((2,)),
         ],
         compiler_params=pltpu.CompilerParams(
-            collective_id=0, has_side_effects=True, vmem_limit_bytes=48 * 2**20
+            collective_id=0, has_side_effects=True, vmem_limit_bytes=60 * 2**20
         ),
     )(
         counts, selected, old_place, new_place,
         acts[0], out_grads[0], next_tokens[0], master[0], first_moment[0], second_moment[0],
     )
+    w, m, v, f = pl.pallas_call(
+        write,
+        out_shape=(state, state, state, jax.ShapeDtypeStruct((TOK, 768), BF16)),
+        in_specs=[anywhere] * 4,
+        out_specs=(anywhere,) * 4,
+        scratch_shapes=[pltpu.VMEM((ROWS, 768), F32)] * 3
+        + [pltpu.VMEM((TOK, 768), BF16), pltpu.SemaphoreType.DMA((2, 4))],
+        compiler_params=pltpu.CompilerParams(vmem_limit_bytes=60 * 2**20),
+    )(w, m, v, f)
     return w[None], m[None], v[None], f[None]
 
 

time: 109 us -> 90.5 us (0.83); the launches traced: 107 us -> 90.3 us
  local copies, waits for them, and re-layouts: 9.88 us -> 0 us
  Pallas kernels: 96.5 us -> 89.7 us
    unnamed x24 -> x0, local copies, waits for them, and re-layouts: 9.88 us -> none
    pallas_call x1, Pallas kernels: 96.5 us -> 87.4 us  [body(): pl.pallas_call(kernel, out_shape=(state, state, state, jax.ShapeDtypeStru...]
    pallas_call x0 -> x1, Pallas kernels: none -> 2.26 us  [body(): pl.pallas_call(write, out_shape=(state, state, state, jax.ShapeDtypeStruc...]
where the time goes in v2:
time: 90.5 us; the launch traced here: 90.3 us
  Pallas kernels  89.7 us (99%)
    pallas_call x1, Pallas kernels, body(): pl.pallas_call(kernel, out_shape=(state, state, state, jax.ShapeDtypeStru...  87.4 us
    pallas_call x1, Pallas kernels, body(): pl.pallas_call(write, out_shape=(state, state, state, jax.ShapeDtypeStruc...  2.26 us

profile of v2, /device:TPU:1, one launch (start us, length us, event | category | flops | bytes accessed | tf_op | source)
XLA Modules:
  0.0 90.3 jit_solution(3332394563588506759)
XLA Ops:
  0.6 87.4 %shard_map.129 = (f32[160,768]{1,0:T(8,128)}, f32[160,768]{1,0:T(8,128)}, f32[160,768]{1,0:T(8,128)}, bf16[128,768]{1,0:T(8,128)(2,1)}) custom-call(s32[1,160]{1,0:T(1,128)} %counts_hbm.1, s32[32]{0:T(128)} %selected_hbm.1, s32[32]{0:T(128)} %old_hbm.1, s32[32]{0:T(128)} %new_hbm.1, bf16[128,2560]{1,0:T(8,128)(2,1)} %bitcast.10, bf16[128,768]{1,0:T(8,128)(2,1)} %bitcast.15, ...), custom_call_target="tpu_custom_call" | custom-call | tf_op jit(solution)/shard_map/pallas_call | solution.py:355
  88.1 2.3 %shard_map.130 = (f32[160,768]{1,0:T(8,128)}, f32[160,768]{1,0:T(8,128)}, f32[160,768]{1,0:T(8,128)}, bf16[128,768]{1,0:T(8,128)(2,1)}) custom-call(f32[160,768]{1,0:T(8,128)} %get-tuple-element.12.w, f32[160,768]{1,0:T(8,128)} %get-tuple-element.13.m, f32[160,768]{1,0:T(8,128)} %get-tuple-element.14.v, bf16[128,768]{1,0:T(8,128)(2,1)} %get-tuple-element.15.f), custom_call_target="tpu_custom_call" | custom-call | tf_op jit(solution)/shard_map/pallas_call | solution.py:414

commit v3 on v2

--- a/solution.py
+++ b/solution.py
@@ -117,7 +117,6 @@
         push(at.at[other, t], at_in.at[k], x_send.at[k], x_recv.at[k], partner)
     reads[6].wait()
     turned(tokens, nt)
-    push(nt.at[other], nt_in, x_send.at[9], x_recv.at[9], partner)
 
     def place(d, c):
         def look(i, c):
@@ -138,6 +137,8 @@
     got(g_in, x_recv.at[8])
     arrived = set()
     for s in range(4):
+        if s == 2:
+            push(nt.at[other], nt_in, x_send.at[9], x_recv.at[9], partner)
         for c, (h, way, hops) in enumerate(CHAINS):
             if s >= hops:
                 continue
@@ -159,16 +160,19 @@
     got(at_in.at[0], x_recv.at[0])
 
     def one_phase_out(stage, relay, send, recv, first_relay):
-        def go(n, c):
-            j = n + first_relay
-
-            @pl.when(j != me)
-            def _():
-                push(stage.at[n], relay.at[me], send, recv, (dp, j))
-
-            return c
-
-        lax.fori_loop(0, RELAYS, go, 0)
+        for lane in range(4):
+
+            def go(z, c, lane=lane):
+                j = 4 * z + lane
+                n = j - first_relay
+
+                @pl.when((j != me) & (n >= 0) & (n < RELAYS))
+                def _():
+                    push(stage.at[n], relay.at[me], send, recv, (dp, j))
+
+                return c
+
+            lax.fori_loop(0, HOLD // 4, go, 0)
 
     for i in (7, 8, 9):
         reads[i].wait()

time: 90.5 us -> 90.1 us (level)
  the two profiles are of different devices: /device:TPU:1 before, /device:TPU:70 now
where the time goes in v3:
time: 90.1 us; the launch traced here: 89.9 us
  Pallas kernels  89.3 us (99%)
    pallas_call x1, Pallas kernels, body(): pl.pallas_call(kernel, out_shape=(state, state, state, jax.ShapeDtypeStru...  87 us
    pallas_call x1, Pallas kernels, body(): pl.pallas_call(write, out_shape=(state, state, state, jax.ShapeDtypeStruc...  2.26 us

profile of v3, /device:TPU:70, one launch (start us, length us, event | category | flops | bytes accessed | tf_op | source)
XLA Modules:
  0.0 89.9 jit_solution(13212656238160266706)
XLA Ops:
  0.6 87.0 %shard_map.129 = (f32[160,768]{1,0:T(8,128)}, f32[160,768]{1,0:T(8,128)}, f32[160,768]{1,0:T(8,128)}, bf16[128,768]{1,0:T(8,128)(2,1)}) custom-call(s32[1,160]{1,0:T(1,128)} %counts_hbm.1, s32[32]{0:T(128)} %selected_hbm.1, s32[32]{0:T(128)} %old_hbm.1, s32[32]{0:T(128)} %new_hbm.1, bf16[128,2560]{1,0:T(8,128)(2,1)} %bitcast.10, bf16[128,768]{1,0:T(8,128)(2,1)} %bitcast.15, ...), custom_call_target="tpu_custom_call" | custom-call | tf_op jit(solution)/shard_map/pallas_call | solution.py:359
  87.6 2.3 %shard_map.130 = (f32[160,768]{1,0:T(8,128)}, f32[160,768]{1,0:T(8,128)}, f32[160,768]{1,0:T(8,128)}, bf16[128,768]{1,0:T(8,128)(2,1)}) custom-call(f32[160,768]{1,0:T(8,128)} %get-tuple-element.12.w, f32[160,768]{1,0:T(8,128)} %get-tuple-element.13.m, f32[160,768]{1,0:T(8,128)} %get-tuple-element.14.v, bf16[128,768]{1,0:T(8,128)(2,1)} %get-tuple-element.15.f), custom_call_target="tpu_custom_call" | custom-call | tf_op jit(solution)/shard_map/pallas_call | solution.py:418

commit v4 on v3

--- a/solution.py
+++ b/solution.py
@@ -251,12 +251,6 @@
     def _():
         relay_m[me] = stage_m[me - 2]
 
-    for p in range(RELAYS):
-        k, q = p // 3, p % 3
-        for h in range(2):
-            cols = slice(h * WIDE + 128 * q, h * WIDE + 128 * q + 128)
-            out_w[16 * k : 16 * k + 16, cols] = new_w[h, p].astype(F32)
-
     got(nt_in, x_recv.at[9])
     for i in range(10):
         ntx[0:128, 128 * i : 128 * i + 128] = jnp.concatenate(
@@ -289,6 +283,12 @@
     for h in range(2):
         whole = gathered[h].reshape(RING * ROWS, WIDE)
         f_own[h] = jnp.dot(ntx[128:256], whole, preferred_element_type=F32)
+
+    for p in range(RELAYS):
+        k, q = p // 3, p % 3
+        for h in range(2):
+            cols = slice(h * WIDE + 128 * q, h * WIDE + 128 * q + 128)
+            out_w[16 * k : 16 * k + 16, cols] = new_w[h, p].astype(F32)
 
     two_phase_in(new_m, p_recv.at[1, 2], 2)
     for p in range(RELAYS):

time: 90.1 us -> 90.1 us (level)
  no operation moved by 1% of the time
where the time goes in v4:
time: 90.1 us; the launch traced here: 89.9 us
  Pallas kernels  89.3 us (99%)
    pallas_call x1, Pallas kernels, body(): pl.pallas_call(kernel, out_shape=(state, state, state, jax.ShapeDtypeStru...  87 us
    pallas_call x1, Pallas kernels, body(): pl.pallas_call(write, out_shape=(state, state, state, jax.ShapeDtypeStruc...  2.26 us

profile of v4, /device:TPU:70, one launch (start us, length us, event | category | flops | bytes accessed | tf_op | source)
XLA Modules:
  0.0 89.9 jit_solution(3057654407200904510)
XLA Ops:
  0.6 87.0 %shard_map.129 = (f32[160,768]{1,0:T(8,128)}, f32[160,768]{1,0:T(8,128)}, f32[160,768]{1,0:T(8,128)}, bf16[128,768]{1,0:T(8,128)(2,1)}) custom-call(s32[1,160]{1,0:T(1,128)} %counts_hbm.1, s32[32]{0:T(128)} %selected_hbm.1, s32[32]{0:T(128)} %old_hbm.1, s32[32]{0:T(128)} %new_hbm.1, bf16[128,2560]{1,0:T(8,128)(2,1)} %bitcast.10, bf16[128,768]{1,0:T(8,128)(2,1)} %bitcast.15, ...), custom_call_target="tpu_custom_call" | custom-call | tf_op jit(solution)/shard_map/pallas_call | solution.py:359
  87.6 2.3 %shard_map.130 = (f32[160,768]{1,0:T(8,128)}, f32[160,768]{1,0:T(8,128)}, f32[160,768]{1,0:T(8,128)}, bf16[128,768]{1,0:T(8,128)(2,1)}) custom-call(f32[160,768]{1,0:T(8,128)} %get-tuple-element.12.w, f32[160,768]{1,0:T(8,128)} %get-tuple-element.13.m, f32[160,768]{1,0:T(8,128)} %get-tuple-element.14.v, bf16[128,768]{1,0:T(8,128)(2,1)} %get-tuple-element.15.f), custom_call_target="tpu_custom_call" | custom-call | tf_op jit(solution)/shard_map/pallas_call | solution.py:418
